TPU v7x, 32 devices: a whole 2x2x4 slice. The times are simulated.
32 devices in a mesh: dp: 8 (over z, x), rep: 4 (over y, core).
Axes of the slice: x: 2, y: 2, z: 4, core: 2. Of those that a mesh axis runs over, the one named last changes fastest.
Arguments:
- features: bfloat16 [3, 20480, 2048], P(None, ('dp', 'rep')), may hold values from -6 to 6
- cotangent: bfloat16 [3, 20480, 2048], P(None, ('dp', 'rep')), may hold values from -6 to 6
- neighbours: int32 [3, 20480, 32], P(None, ('dp', 'rep')), may hold values from 0 to 127
- segments: int32 [3, 20480], P(None, ('dp', 'rep')), may hold values from 0 to 639, never falling along the last dimension, each value on 1 to 64 neighbouring positions
- live: int32 [3, 20480], P(None, ('dp', 'rep')), may hold values 0 or 1
- weight: bfloat16 [2048, 2048], P(('dp', 'rep')), may hold values from -0.125 to 0.125
- bias: bfloat16 [2048], P(('dp', 'rep')), may hold values from -3 to 3
Outputs:
- activations: bfloat16 [3, 20480, 2048], P(None, ('dp', 'rep'))
- feature_grad: bfloat16 [3, 20480, 2048], P(None, ('dp', 'rep'))
- weight_grad: float32 [2048, 2048], P(('dp', 'rep'))
- bias_grad: float32 [2048], P(('dp', 'rep'))
Inputs may be any that keep to these rules, and one draw needn't show every extreme that they name: `neighbours`: positions within the node's own slot of 128 nodes. `segments`: never falling along the nodes of a micro-batch; each cluster has 1 to 64 nodes, one exactly 64.
All inputs are finite; a program needn't handle non-finite values. No bound on the sum of `live` on one device may be relied on, other than what follows from the above.
Results may differ from a plain program's by a relative error of at most 0.0055.
Values may be sent and summed in bfloat16 or wider, within the bound.
A program may use at most 192 MiB of HBM per device.

v0:
```python
import functools

import jax
import jax.numpy as jnp
from jax import lax
from jax.experimental import pallas as pl
from jax.experimental.pallas import tpu as pltpu
from jax.sharding import PartitionSpec as P

SLOT = 128
LANES = 128
CHUNK = 256
RING = 4
MESH = pl.DeviceIdType.MESH
F32, BF16 = jnp.float32, jnp.bfloat16
ENHANCE = 1.0


def split_axes(dp, rep):
    b = 2 ** ((dp.bit_length() - 1) // 2)
    return dp // b, b, rep // 2, 2


def kernel(
    dims, feat, cot, nbr, seg, live, weight, bias, act_out, fgrad_out, wgrad_out, bgrad_out,
    wg, pool, pool_t, gp, ct, act, acc, csend, crecv, s1a, s1b, s2a, s2b, sz, r1a, r1b, r2a, r2b, rz,
    nbuf, sbuf, lbuf, adj_t, scale, fout, wout, bb, brow, bacc, bt, bsum, brc, br1, br2, brz,
    in_sem, ct_sem, act_sem, fout_sem, wout_sem,
    gz_s, gz_r, g1a_s, g1a_r, g1b_s, g1b_r, g2a_s, g2a_r, g2b_s, g2b_r, gc_s, gc_r,
    rc_s, rc_r, p1a_s, p1a_r, p1b_s, p1b_r, p2a_s, p2a_r, p2b_s, p2b_r, pz_s, pz_r,
    bz_s, bz_r, b1_s, b1_r, b2_s, b2_r, bc_s, bc_r, dc_s, dc_r, d1_s, d1_r, d2_s, d2_r, dz_s, dz_r,
):
    A, B, Y, C = dims
    batches, local, D = feat.shape
    rows = weight.shape[0]
    slots = local // SLOT
    N = batches * local
    chunks = D // CHUNK
    groups = A * B * Y
    plane = groups * rows
    wide = D // A
    half = N // 2

    dp, rep = lax.axis_index("dp"), lax.axis_index("rep")
    a, b, y, c = lax.div(dp, B), lax.rem(dp, B), lax.div(rep, C), lax.rem(rep, C)
    oc = 1 - c

    def device(a_, b_, y_, c_):
        return (a_ * B + b_, y_ * C + c_)

    def up(v, d, n):
        return lax.rem(v + d, n)

    def down(v, d, n):
        return lax.rem(v + n - d, n)

    to_a = [(d, device(up(a, d, A), b, y, c)) for d in range(1, A)]
    to_b = [(d, device(a, up(b, d, B), y, c)) for d in range(1, B)]
    to_y = [(d, device(a, b, up(y, d, Y), c)) for d in range(1, Y)]
    to_c = device(a, b, y, oc)

    def remote(src, dst, ssem, rsem, dev):
        return pltpu.make_async_remote_copy(
            src_ref=src, dst_ref=dst, send_sem=ssem, recv_sem=rsem, device_id=dev, device_id_type=MESH
        )

    weight_loads = [
        pltpu.make_async_copy(
            weight.at[:, pl.ds((2 * k + h) * LANES, LANES)], wg.at[k, h, a, b, y, c], in_sem.at[0, k * 2 + h]
        )
        for k in range(chunks)
        for h in range(2)
    ]
    side_loads = [
        pltpu.make_async_copy(nbr, nbuf, in_sem.at[1, 0]),
        pltpu.make_async_copy(seg, sbuf, in_sem.at[1, 1]),
        pltpu.make_async_copy(live, lbuf, in_sem.at[1, 2]),
    ]
    bias_load = pltpu.make_async_copy(bias, bb.at[a, b, y, c], in_sem.at[1, 3])
    feat_loads = [
        pltpu.make_async_copy(feat.at[m], gp.at[pl.ds(m * local, local)], in_sem.at[1, 4 + m]) for m in range(batches)
    ]
    for copy in weight_loads:
        copy.start()
    bias_load.start()
    for copy in side_loads:
        copy.start()
    for copy in feat_loads:
        copy.start()

    barrier = pltpu.get_barrier_semaphore()
    partners = [dev for _, dev in to_a + to_b + to_y] + [to_c]
    for dev in partners:
        pl.semaphore_signal(barrier, inc=1, device_id=dev, device_id_type=MESH)

    def cot_load(k, m):
        return pltpu.make_async_copy(
            cot.at[m, :, pl.ds(pl.multiple_of(k * CHUNK, CHUNK), CHUNK)],
            ct.at[lax.rem(k, 2), pl.ds(m * local, local)],
            ct_sem.at[lax.rem(k, 2), m],
        )

    def act_store(k, m):
        return pltpu.make_async_copy(
            act.at[lax.rem(k, 2), pl.ds(m * local, local)],
            act_out.at[m, :, pl.ds(pl.multiple_of(k * CHUNK, CHUNK), CHUNK)],
            act_sem.at[lax.rem(k, 2), m],
        )

    pl.semaphore_wait(barrier, len(partners))

    def gather_z(k, d, dev, mine):
        at = a if mine else down(a, d, A)
        ref = wg.at[k, :, at, b, y, c]
        return remote(ref, ref, gz_s.at[k, d - 1], gz_r.at[k, d - 1], dev)

    def gather_1(k, mine):
        out = []
        for d, dev in to_b:
            ref = wg.at[k, 0, :, b if mine else down(b, d, B), y, c]
            out.append(remote(ref, ref, g1a_s.at[k, d - 1], g1a_r.at[k, d - 1], dev))
        for d, dev in to_y:
            ref = wg.at[k, 1, :, b, y if mine else down(y, d, Y), c]
            out.append(remote(ref, ref, g1b_s.at[k, d - 1], g1b_r.at[k, d - 1], dev))
        return out

    def gather_2(k, mine):
        out = []
        for d, dev in to_y:
            ref = wg.at[k, 0, :, :, y if mine else down(y, d, Y), c]
            out.append(remote(ref, ref, g2a_s.at[k, d - 1], g2a_r.at[k, d - 1], dev))
        for d, dev in to_b:
            ref = wg.at[k, 1, :, b if mine else down(b, d, B), :, c]
            out.append(remote(ref, ref, g2b_s.at[k, d - 1], g2b_r.at[k, d - 1], dev))
        return out

    def gather_c(k, mine):
        ref = wg.at[k, :, :, :, :, c if mine else oc]
        return remote(ref, ref, gc_s.at[k], gc_r.at[k], to_c)

    def guarded(fn):
        def at(k):
            if isinstance(k, int):
                if 0 <= k < chunks:
                    fn(k)
            else:
                pl.when(jnp.logical_and(k >= 0, k < chunks))(lambda: fn(k))

        return at

    def bias_z(d, dev, mine):
        ref = bb.at[a if mine else down(a, d, A), b, y, c]
        return remote(ref, ref, bz_s.at[d - 1], bz_r.at[d - 1], dev)

    def bias_1(d, dev, mine):
        ref = bb.at[:, b if mine else down(b, d, B), y, c]
        return remote(ref, ref, b1_s.at[d - 1], b1_r.at[d - 1], dev)

    def bias_2(d, dev, mine):
        ref = bb.at[:, :, y if mine else down(y, d, Y), c]
        return remote(ref, ref, b2_s.at[d - 1], b2_r.at[d - 1], dev)

    def bias_c(mine):
        ref = bb.at[:, :, :, c if mine else oc]
        return remote(ref, ref, bc_s.at[0], bc_r.at[0], to_c)

    @guarded
    def ag1(k):
        for d, dev in to_a:
            gather_z(k, d, dev, False).wait_recv()
        for copy in gather_1(k, True):
            copy.start()

    @guarded
    def ag2(k):
        for copy in gather_1(k, False):
            copy.wait_recv()
        for copy in gather_2(k, True):
            copy.start()

    @guarded
    def ag3(k):
        for copy in gather_2(k, False):
            copy.wait_recv()
        gather_c(k, True).start()

    def bias_ag1():
        for d, dev in to_a:
            bias_z(d, dev, False).wait_recv()
        for d, dev in to_b:
            bias_1(d, dev, True).start()

    def bias_ag2():
        for d, dev in to_b:
            bias_1(d, dev, False).wait_recv()
        for d, dev in to_y:
            bias_2(d, dev, True).start()

    def bias_ag3():
        for d, dev in to_y:
            bias_2(d, dev, False).wait_recv()
        bias_c(True).start()

    for copy in weight_loads[:2]:
        copy.wait()
    bias_load.wait()
    for d, dev in to_a:
        gather_z(0, d, dev, True).start()
        bias_z(d, dev, True).start()
    for copy in weight_loads[2:]:
        copy.wait()
    for k in range(1, chunks):
        for d, dev in to_a:
            gather_z(k, d, dev, True).start()

    for copy in side_loads:
        copy.wait()
    for m in range(batches):
        cot_load(0, m).start()
    bacc[...] = jnp.zeros_like(bacc)

    def pooling(m, q):
        s = m * slots + q
        here = pl.multiple_of(q * SLOT, SLOT)
        flat = pl.multiple_of(s * SLOT, SLOT)
        lists = nbuf[m, pl.ds(here, SLOT), :]
        lane = lax.broadcasted_iota(jnp.int32, (SLOT, SLOT), 1)
        sub = lax.broadcasted_iota(jnp.int32, (SLOT, SLOT), 0)
        reps = SLOT // lists.shape[1]
        listed = jnp.concatenate([lists] * reps, axis=1).astype(F32).T.astype(BF16)
        position = sub.astype(F32).astype(BF16)
        counted = jnp.zeros((SLOT, SLOT), BF16)
        for j in range(lists.shape[1]):
            counted = counted + jnp.where(listed[j : j + 1, :] == position, jnp.bfloat16(1), jnp.bfloat16(0))
        counted = counted.astype(F32).T
        ids, alive = sbuf[m : m + 1, pl.ds(here, SLOT)], lbuf[m : m + 1, pl.ds(here, SLOT)]
        along = jnp.where(alive > 0, ids, -1)
        down_ = jnp.broadcast_to(jnp.where(alive > 0, ids, -2), (SLOT, SLOT)).T
        adjacency = jnp.where(down_ == along, counted, 0.0)
        degree = jnp.sum(adjacency, axis=1, keepdims=True)
        factor = jnp.where(down_ >= 0, 1.0 / (degree + 1.0), 0.0)
        adjacency = jnp.where(lane == sub, (1.0 + ENHANCE) * (adjacency + 1.0), adjacency)
        adj_t[s] = adjacency.T.astype(BF16)
        scale[pl.ds(flat, SLOT), :] = factor
        pooled = jnp.dot(adjacency.astype(BF16), gp[pl.ds(flat, SLOT), :], preferred_element_type=F32)
        pooled = (pooled * jnp.concatenate([factor] * (D // SLOT), axis=1)).astype(BF16)
        pool[pl.ds(flat, SLOT), :] = pooled
        pool_t[:, :, :, pl.ds(flat, SLOT)] = pooled.T.reshape(groups, C, rows, SLOT)

    early = {
        4: [lambda: ag1(0), bias_ag1],
        7: [lambda: ag1(1)],
        8: [lambda: ag2(0), bias_ag2],
        10: [lambda: ag1(2)],
        11: [lambda: ag2(1)],
        13: [lambda: ag3(0), bias_ag3, lambda: ag1(3)],
    }
    for m in range(batches):
        feat_loads[m].wait()

        def step(q, carry, m=m):
            pooling(m, q)
            for at, events in early.items():
                if m * slots <= at < (m + 1) * slots:

                    @pl.when(q == at - m * slots)
                    def _(events=events):
                        for event in events:
                            event()

            return carry

        lax.fori_loop(0, slots, step, 0)

    bias_c(False).wait_recv()
    tiles = bb[...].reshape(groups * C, 8, LANES)
    per = LANES // rows
    owner = lax.div(lax.broadcasted_iota(jnp.int32, (1, LANES), 1), rows)
    for j in range(D // LANES):
        row = jnp.zeros((1, LANES), F32)
        for p in range(per):
            row = jnp.where(owner == p, tiles[j * per + p, 0:1, :], row)
        brow[j] = jnp.broadcast_to(row, (8, LANES))

    def reduce_c(k):
        return remote(csend.at[lax.rem(k, 2)], crecv.at[k], rc_s.at[k], rc_r.at[k], to_c)

    def reduce_1(k):
        e = lax.rem(k, 2)
        out_a = [
            remote(s1a.at[e, d - 1], r1a.at[k, d - 1], p1a_s.at[k, d - 1], p1a_r.at[k, d - 1], dev) for d, dev in to_y
        ]
        out_b = [
            remote(s1b.at[e, d - 1], r1b.at[k, d - 1], p1b_s.at[k, d - 1], p1b_r.at[k, d - 1], dev) for d, dev in to_b
        ]
        return out_a + out_b

    def reduce_2(k):
        e = lax.rem(k, 2)
        out_a = [
            remote(s2a.at[e, d - 1], r2a.at[k, d - 1], p2a_s.at[k, d - 1], p2a_r.at[k, d - 1], dev) for d, dev in to_b
        ]
        out_b = [
            remote(s2b.at[e, d - 1], r2b.at[k, d - 1], p2b_s.at[k, d - 1], p2b_r.at[k, d - 1], dev) for d, dev in to_y
        ]
        return out_a + out_b

    def reduce_z(k):
        e = lax.rem(k, 2)
        return [remote(sz.at[e, d - 1], rz.at[k, d - 1], pz_s.at[k, d - 1], pz_r.at[k, d - 1], dev) for d, dev in to_a]

    def ago(k, n, copies):
        def wait():
            for copy in copies(k - n):
                copy.wait_send()

        if isinstance(k, int):
            if k >= n:
                wait()
        else:
            pl.when(k >= n)(wait)

    lo, hi = slice(0, LANES), slice(LANES, CHUNK)

    @guarded
    def rs1(k):
        t, e = lax.rem(k, RING), lax.rem(k, 2)
        reduce_c(k).wait_recv()
        ago(k, 2, reduce_1)
        for d, _ in to_y:
            v = up(y, d, Y)
            s1a[e, d - 1] = (acc[t, :, :, v, :, lo] + crecv[k, :, :, v, :, lo].astype(F32)).astype(BF16)
        for d, _ in to_b:
            v = up(b, d, B)
            s1b[e, d - 1] = (acc[t, :, v, :, :, hi] + crecv[k, :, v, :, :, hi].astype(F32)).astype(BF16)
        for copy in reduce_1(k):
            copy.start()
        acc[t, :, :, y, :, lo] = acc[t, :, :, y, :, lo] + crecv[k, :, :, y, :, lo].astype(F32)
        acc[t, :, b, :, :, hi] = acc[t, :, b, :, :, hi] + crecv[k, :, b, :, :, hi].astype(F32)

    @guarded
    def rs2(k):
        t, e = lax.rem(k, RING), lax.rem(k, 2)
        for copy in reduce_1(k):
            copy.wait_recv()
        ago(k, 2, reduce_2)

        def total_a(v):
            out = acc[t, :, v, y, :, lo]
            for d, _ in to_y:
                out = out + r1a[k, d - 1, :, v].astype(F32)
            return out

        def total_b(v):
            out = acc[t, :, b, v, :, hi]
            for d, _ in to_b:
                out = out + r1b[k, d - 1, :, v].astype(F32)
            return out

        for d, _ in to_b:
            s2a[e, d - 1] = total_a(up(b, d, B)).astype(BF16)
        for d, _ in to_y:
            s2b[e, d - 1] = total_b(up(y, d, Y)).astype(BF16)
        for copy in reduce_2(k):
            copy.start()
        acc[t, :, b, y, :, lo] = total_a(b)
        acc[t, :, b, y, :, hi] = total_b(y)

    @guarded
    def rs3(k):
        t, e = lax.rem(k, RING), lax.rem(k, 2)
        for copy in reduce_2(k):
            copy.wait_recv()
        ago(k, 2, reduce_z)

        def total(v):
            left, right = acc[t, v, b, y, :, lo], acc[t, v, b, y, :, hi]
            for d, _ in to_b:
                left = left + r2a[k, d - 1, v].astype(F32)
            for d, _ in to_y:
                right = right + r2b[k, d - 1, v].astype(F32)
            return jnp.concatenate([left, right], axis=1)

        for d, _ in to_a:
            sz[e, d - 1] = total(up(a, d, A)).astype(BF16)
        for copy in reduce_z(k):
            copy.start()
        acc[t, a, b, y] = total(a)

    def wout_store(k):
        cols = pl.ds(pl.multiple_of(k * CHUNK, CHUNK), CHUNK)
        return pltpu.make_async_copy(wout.at[k], wgrad_out.at[:, cols], wout_sem.at[k])

    @guarded
    def rs4(k):
        t = lax.rem(k, RING)
        for copy in reduce_z(k):
            copy.wait_recv()
        out = acc[t, a, b, y]
        for d, _ in to_a:
            out = out + rz[k, d - 1].astype(F32)
        wout[k] = out
        wout_store(k).start()

    def columns(k):
        return pl.ds(pl.multiple_of(k * CHUNK, CHUNK), CHUNK)

    def forward(k, i):
        e = lax.rem(k, 2)
        part = pl.ds(i * half, half)
        w = jnp.concatenate([wg[k, h].reshape(D, LANES) for h in range(2)], axis=1)
        offset = jnp.concatenate([brow[2 * k + h][0:1] for h in range(2)], axis=1)
        preact = jnp.dot(pool[part, :], w, preferred_element_type=F32) + offset
        squash = jax.nn.sigmoid(preact)
        active = preact * squash
        act[e, part, :] = active.astype(BF16)
        grad = (ct[e, part, :].astype(F32) * (squash + active * (1.0 - squash))).astype(BF16)
        gp[part, columns(k)] = grad
        bacc[:, columns(k)] += jnp.sum(grad.astype(F32).reshape(half // 8, 8, CHUNK), axis=0)

    def weight_term(k, which):
        left = pool_t[:, which].reshape(plane, N)
        return jnp.dot(left, gp[:, columns(k)], preferred_element_type=F32).reshape(A, B, Y, rows, CHUNK)

    def chunk(k, carry):
        e, t = lax.rem(k, 2), lax.rem(k, RING)
        gather_c(k, False).wait_recv()
        for m in range(batches):
            cot_load(k, m).wait()

        @pl.when(k + 1 < chunks)
        def _():
            for m in range(batches):
                cot_load(k + 1, m).start()

        @pl.when(k >= 2)
        def _():
            for m in range(batches):
                act_store(k - 2, m).wait()

        pl.when(k >= 0)(lambda: forward(k, 0))
        ag2(k + 2)
        ag3(k + 1)
        rs1(k - 1)
        rs4(k - 4)
        pl.when(k >= 0)(lambda: forward(k, 1))
        for m in range(batches):
            act_store(k, m).start()
        rs2(k - 2)
        ago(k, 2, lambda j: [reduce_c(j)])

        @pl.when(k >= 0)
        def _():
            csend[e] = weight_term(k, oc).astype(BF16)

        reduce_c(k).start()
        ag1(k + 4)
        rs3(k - 3)

        @pl.when(k >= 0)
        def _():
            acc[t] = weight_term(k, c)

        return carry

    lax.fori_loop(0, chunks, chunk, 0)

    def bred_c():
        return remote(bt.at[:, :, :, oc], brc, dc_s.at[0], dc_r.at[0], to_c)

    def bred_1():
        return [remote(bsum.at[:, :, up(y, d, Y)], br1.at[d - 1], d1_s.at[d - 1], d1_r.at[d - 1], dev) for d, dev in to_y]

    def bred_2():
        return [remote(bsum.at[:, up(b, d, B), y], br2.at[d - 1], d2_s.at[d - 1], d2_r.at[d - 1], dev) for d, dev in to_b]

    def bred_z():
        return [remote(bsum.at[up(a, d, A), b, y], brz.at[d - 1], dz_s.at[d - 1], dz_r.at[d - 1], dev) for d, dev in to_a]

    for a_ in range(A):
        for b_ in range(B):
            for y_ in range(Y):
                for c_ in range(C):
                    block = (((a_ * B + b_) * Y + y_) * C + c_) * rows // LANES
                    bt[a_, b_, y_, c_] = bacc[:, block * LANES : (block + 1) * LANES]
    bred_c().start()

    def bias_rs1():
        bred_c().wait_recv()
        bsum[...] = bt[:, :, :, c] + brc[...]
        for copy in bred_1():
            copy.start()

    def bias_rs2():
        for copy in bred_1():
            copy.wait_recv()
        for d, _ in to_y:
            bsum[:, :, y] = bsum[:, :, y] + br1[d - 1]
        for copy in bred_2():
            copy.start()

    def bias_rs3():
        for copy in bred_2():
            copy.wait_recv()
        for d, _ in to_b:
            bsum[:, b, y] = bsum[:, b, y] + br2[d - 1]
        for copy in bred_z():
            copy.start()

    def bias_rs4():
        for copy in bred_z():
            copy.wait_recv()
        out = bsum[a, b, y]
        for d, _ in to_a:
            out = out + brz[d - 1]
        out = jnp.sum(out, axis=0, keepdims=True)
        place = lax.rem((dp * (Y * C) + rep) * rows, LANES)
        mine = jnp.zeros((1, rows), F32)
        for p in range(per):
            mine = jnp.where(place == p * rows, out[:, p * rows : (p + 1) * rows], mine)
        bgrad_out[...] = mine

    def fout_store(i):
        return pltpu.make_async_copy(
            fout.at[lax.rem(i, 2)],
            fgrad_out.at[lax.rem(i, batches), :, pl.ds(pl.multiple_of(lax.div(i, batches) * wide, wide), wide)],
            fout_sem.at[lax.rem(i, 2)],
        )

    def feature_grad(i):
        e, n, m = lax.rem(i, 2), lax.div(i, batches), lax.rem(i, batches)
        base = pl.multiple_of(m * local, local)
        w = jnp.concatenate([wg[k, h, n].reshape(wide, LANES) for k in range(chunks) for h in range(2)], axis=1)
        grad = lax.dot_general(gp[pl.ds(base, local), :], w, (((1,), (1,)), ((), ())), preferred_element_type=F32)
        grad = grad * jnp.concatenate([scale[pl.ds(base, local), :]] * (wide // LANES), axis=1)
        high = grad.astype(BF16)
        low = (grad - high.astype(F32)).astype(BF16)
        for q in range(slots):
            left = adj_t[m * slots + q]
            part = slice(q * SLOT, (q + 1) * SLOT)
            right = jnp.concatenate([high[part], low[part]], axis=0)
            out = jnp.dot(jnp.concatenate([left, left], axis=1), right, preferred_element_type=F32)
            fout[e, part, :] = out.astype(BF16)

    late = {
        0: [lambda: rs1(chunks - 1), bias_rs1, lambda: rs2(chunks - 2), lambda: rs3(chunks - 3), lambda: rs4(chunks - 4)],
        2: [lambda: rs2(chunks - 1), bias_rs2, lambda: rs3(chunks - 2), lambda: rs4(chunks - 3)],
        5: [lambda: rs3(chunks - 1), bias_rs3, lambda: rs4(chunks - 2)],
        8: [lambda: rs4(chunks - 1), bias_rs4],
    }
    steps = A * batches

    def last(i, carry):
        @pl.when(i >= 2)
        def _():
            fout_store(i - 2).wait()

        pl.when(i >= 0)(lambda: feature_grad(i))
        fout_store(i).start()
        for at, events in late.items():

            @pl.when(i == at)
            def _(events=events):
                for event in events:
                    event()

        return carry

    lax.fori_loop(0, steps, last, 0)

    for i in (steps - 2, steps - 1):
        fout_store(i).wait()
    for k in (chunks - 2, chunks - 1):
        for m in range(batches):
            act_store(k, m).wait()
        for copy in [reduce_c(k)] + reduce_1(k) + reduce_2(k) + reduce_z(k):
            copy.wait_send()

    def drained(k, carry):
        wout_store(k).wait()
        for d, dev in to_a:
            gather_z(k, d, dev, True).wait_send()
        for copy in gather_1(k, True) + gather_2(k, True) + [gather_c(k, True)]:
            copy.wait_send()
        return carry

    lax.fori_loop(0, chunks, drained, 0)
    for d, dev in to_a:
        bias_z(d, dev, True).wait_send()
    for d, dev in to_b:
        bias_1(d, dev, True).wait_send()
    for d, dev in to_y:
        bias_2(d, dev, True).wait_send()
    bias_c(True).wait_send()
    for copy in [bred_c()] + bred_1() + bred_2() + bred_z():
        copy.wait_send()


def per_device(dims, features, cotangent, neighbours, segments, live, weight, bias):
    A, B, Y, C = dims
    batches, local, D = features.shape
    rows = weight.shape[0]
    N = batches * local
    chunks = D // CHUNK
    groups = A * B * Y
    wide = D // A
    tile = jnp.broadcast_to(jnp.tile(bias.astype(F32), LANES // rows)[None], (8, LANES))
    any_spec = pl.BlockSpec(memory_space=pl.ANY)
    vmem, dma = pltpu.VMEM, pltpu.SemaphoreType.DMA
    scratch = [
        vmem((chunks, 2, A, B, Y, C, rows, LANES), BF16),
        vmem((N, D), BF16),
        vmem((groups, C, rows, N), BF16),
        vmem((N, D), BF16),
        vmem((2, N, CHUNK), BF16),
        vmem((2, N, CHUNK), BF16),
        vmem((RING, A, B, Y, rows, CHUNK), F32),
        vmem((2, A, B, Y, rows, CHUNK), BF16),
        vmem((chunks, A, B, Y, rows, CHUNK), BF16),
        vmem((2, Y - 1, A, B, rows, LANES), BF16),
        vmem((2, B - 1, A, Y, rows, LANES), BF16),
        vmem((2, B - 1, A, rows, LANES), BF16),
        vmem((2, Y - 1, A, rows, LANES), BF16),
        vmem((2, A - 1, rows, CHUNK), BF16),
        vmem((chunks, Y - 1, A, B, rows, LANES), BF16),
        vmem((chunks, B - 1, A, Y, rows, LANES), BF16),
        vmem((chunks, B - 1, A, rows, LANES), BF16),
        vmem((chunks, Y - 1, A, rows, LANES), BF16),
        vmem((chunks, A - 1, rows, CHUNK), BF16),
        vmem(neighbours.shape, jnp.int32),
        vmem(segments.shape, jnp.int32),
        vmem(live.shape, jnp.int32),
        vmem((N // SLOT, SLOT, SLOT), BF16),
        vmem((N, SLOT), F32),
        vmem((2, local, wide), BF16),
        vmem((chunks, rows, CHUNK), F32),
        vmem((A, B, Y, C, 8, LANES), F32),
        vmem((D // LANES, 8, LANES), F32),
        vmem((8, D), F32),
        vmem((A, B, Y, C, 8, LANES), F32),
        vmem((A, B, Y, 8, LANES), F32),
        vmem((A, B, Y, 8, LANES), F32),
        vmem((Y - 1, A, B, 8, LANES), F32),
        vmem((B - 1, A, 8, LANES), F32),
        vmem((A - 1, 8, LANES), F32),
        dma((2, 2 * chunks)),
        dma((2, batches)),
        dma((2, batches)),
        dma((2,)),
        dma((chunks,)),
    ]
    for shape in (
        [(chunks, A - 1), (chunks, B - 1), (chunks, Y - 1), (chunks, Y - 1), (chunks, B - 1), (chunks,)]
        + [(chunks,), (chunks, Y - 1), (chunks, B - 1), (chunks, B - 1), (chunks, Y - 1), (chunks, A - 1)]
        + [(A - 1,), (B - 1,), (Y - 1,), (1,)]
        + [(1,), (Y - 1,), (B - 1,), (A - 1,)]
    ):
        scratch += [dma(shape), dma(shape)]
    act, fgrad, wgrad, bgrad = pl.pallas_call(
        functools.partial(kernel, dims),
        out_shape=[
            jax.ShapeDtypeStruct(features.shape, BF16),
            jax.ShapeDtypeStruct(features.shape, BF16),
            jax.ShapeDtypeStruct(weight.shape, F32),
            jax.ShapeDtypeStruct((1, rows), F32),
        ],
        in_specs=[any_spec] * 7,
        out_specs=[any_spec] * 3 + [pl.BlockSpec(memory_space=pltpu.VMEM)],
        scratch_shapes=scratch,
        compiler_params=pltpu.CompilerParams(
            collective_id=0, has_side_effects=True, vmem_limit_bytes=62 * 2**20
        ),
        cost_estimate=pl.CostEstimate(
            flops=6 * N * D * D, bytes_accessed=8 * N * D, transcendentals=N * D
        ),
    )(features, cotangent, neighbours, segments, live, weight, tile)
    return act, fgrad, wgrad, bgrad.reshape(rows)


def solution(mesh):
    both = ("dp", "rep")
    dims = split_axes(mesh.shape["dp"], mesh.shape["rep"])
    return jax.shard_map(
        functools.partial(per_device, dims),
        mesh=mesh,
        in_specs=(
            P(None, both, None), P(None, both, None), P(None, both, None),
            P(None, both), P(None, both), P(both, None), P(both),
        ),
        out_specs=(P(None, both, None), P(None, both, None), P(both, None), P(both)),
        check_vma=False,
    )
```

profile of v0, /device:TPU:0, one launch (start us, length us, event | category | flops | bytes accessed | tf_op | source)
XLA Modules:
  0.0 126.5 jit_solution(12468407477214576488)
XLA Ops:
  0.6 0.7 tile.2
  1.3 0.1 broadcast_in_dim.7
  1.4 0.6 broadcast_in_dim.8.bias
  2.0 2.2 %copy.11.nbr = s32[3,640,32]{2,1,0:T(8,128)} copy(s32[3,640,32]{1,2,0:T(8,128)} %param.9) | data formatting | bytes 491520 | tf_op args[2]
  4.2 109.6 %shard_map.102 = (bf16[3,640,2048]{2,1,0:T(8,128)(2,1)}, bf16[3,640,2048]{2,1,0:T(8,128)(2,1)}, f32[64,2048]{1,0:T(8,128)}, f32[1,64]{1,0:T(1,128)}) custom-call(bf16[3,640,2048]{2,1,0:T(8,128)(2,1)} %feat.1, bf16[3,640,2048]{2,1,0:T(8,128)(2,1)} %cot.1, s32[3,640,32]{2,1,0:T(8,128)} %copy.11.nbr, s32[3,640]{1,0:T(4,128)} %seg.1, s32[3,640]{1,0:T(4,128)} %live.1, ...), custom_call_target="tpu_custom_call" | custom-call | flops 48318382080 | bytes 31457280 | tf_op jit(solution)/shard_map/pallas_call | solution.py:659
  113.8 0.0 copy-start
  113.8 8.1 %copy.16 = bf16[3,640,2048]{2,1,0:T(8,128)(2,1)} copy(bf16[3,640,2048]{2,1,0:T(8,128)(2,1)} %get-tuple-element.16) | data formatting | bytes 15728640
  121.9 0.0 copy-done
  121.9 0.0 copy-start.1
  121.9 0.0 copy-start.2
  121.9 3.2 %copy.17 = bf16[3,640,2048]{2,1,0:T(8,128)(2,1)} copy(bf16[3,640,2048]{2,1,0:T(8,128)(2,1)S(1)} %copy-done) | data formatting | bytes 15728640
  125.1 0.0 copy-done.1
  125.1 0.8 copy.18
  125.9 0.0 copy-done.2
  125.9 0.5 copy.19
Async XLA Ops:
  113.8 8.1 %copy-start = (bf16[3,640,2048]{2,1,0:T(8,128)(2,1)S(1)}, bf16[3,640,2048]{2,1,0:T(8,128)(2,1)}, u32[]{:S(2)}) copy-start(bf16[3,640,2048]{2,1,0:T(8,128)(2,1)} %get-tuple-element.17) | copy-start | bytes 23592964
  121.9 3.2 %copy-start.1 = (f32[64,2048]{1,0:T(8,128)S(1)}, f32[64,2048]{1,0:T(8,128)}, u32[]{:S(2)}) copy-start(f32[64,2048]{1,0:T(8,128)} %get-tuple-element.18) | copy-start | bytes 1572868
  121.9 4.0 %copy-start.2 = (f32[1,64]{1,0:T(1,128)S(1)}, f32[1,64]{1,0:T(1,128)}, u32[]{:S(2)}) copy-start(f32[1,64]{1,0:T(1,128)} %get-tuple-element.11) | copy-start | bytes 772
where the time goes:
time: 127 us; the launch traced here: 126 us
  Pallas kernels  110 us (87%)
  local copies, waits for them, and re-layouts  16.2 us (13%)
    pallas_call x1, Pallas kernels, per_device(): pl.pallas_call(functools.partial(kernel, dims), out_shape=[jax.ShapeDtype...  110 us
    unnamed x11, local copies, waits for them, and re-layouts  14.9 us

commit v1 on v0

--- a/solution.py
+++ b/solution.py
@@ -10,7 +10,6 @@
 SLOT = 128
 LANES = 128
 CHUNK = 256
-RING = 4
 MESH = pl.DeviceIdType.MESH
 F32, BF16 = jnp.float32, jnp.bfloat16
 ENHANCE = 1.0
@@ -39,7 +38,6 @@
     groups = A * B * Y
     plane = groups * rows
     wide = D // A
-    half = N // 2
 
     dp, rep = lax.axis_index("dp"), lax.axis_index("rep")
     a, b, y, c = lax.div(dp, B), lax.rem(dp, B), lax.div(rep, C), lax.rem(rep, C)
@@ -47,6 +45,9 @@
 
     def device(a_, b_, y_, c_):
         return (a_ * B + b_, y_ * C + c_)
+
+    def columns(k):
+        return pl.ds(k * CHUNK, CHUNK)
 
     def up(v, d, n):
         return lax.rem(v + d, n)
@@ -76,13 +77,11 @@
         pltpu.make_async_copy(seg, sbuf, in_sem.at[1, 1]),
         pltpu.make_async_copy(live, lbuf, in_sem.at[1, 2]),
     ]
-    bias_load = pltpu.make_async_copy(bias, bb.at[a, b, y, c], in_sem.at[1, 3])
     feat_loads = [
         pltpu.make_async_copy(feat.at[m], gp.at[pl.ds(m * local, local)], in_sem.at[1, 4 + m]) for m in range(batches)
     ]
     for copy in weight_loads:
         copy.start()
-    bias_load.start()
     for copy in side_loads:
         copy.start()
     for copy in feat_loads:
@@ -93,60 +92,45 @@
     for dev in partners:
         pl.semaphore_signal(barrier, inc=1, device_id=dev, device_id_type=MESH)
 
-    def cot_load(k, m):
-        return pltpu.make_async_copy(
-            cot.at[m, :, pl.ds(pl.multiple_of(k * CHUNK, CHUNK), CHUNK)],
-            ct.at[lax.rem(k, 2), pl.ds(m * local, local)],
-            ct_sem.at[lax.rem(k, 2), m],
-        )
-
-    def act_store(k, m):
-        return pltpu.make_async_copy(
-            act.at[lax.rem(k, 2), pl.ds(m * local, local)],
-            act_out.at[m, :, pl.ds(pl.multiple_of(k * CHUNK, CHUNK), CHUNK)],
-            act_sem.at[lax.rem(k, 2), m],
-        )
+    def cot_load(k):
+        return pltpu.make_async_copy(cot.at[:, :, columns(k)], ct.at[k % 2], ct_sem.at[k % 2])
+
+    def act_store(k):
+        return pltpu.make_async_copy(act.at[k % 2], act_out.at[:, :, columns(k)], act_sem.at[k % 2])
 
     pl.semaphore_wait(barrier, len(partners))
 
     def gather_z(k, d, dev, mine):
         at = a if mine else down(a, d, A)
         ref = wg.at[k, :, at, b, y, c]
-        return remote(ref, ref, gz_s.at[k, d - 1], gz_r.at[k, d - 1], dev)
+        return remote(ref, ref, gz_s.at[d - 1], gz_r.at[k, d - 1], dev)
 
     def gather_1(k, mine):
         out = []
         for d, dev in to_b:
             ref = wg.at[k, 0, :, b if mine else down(b, d, B), y, c]
-            out.append(remote(ref, ref, g1a_s.at[k, d - 1], g1a_r.at[k, d - 1], dev))
+            out.append(remote(ref, ref, g1a_s.at[d - 1], g1a_r.at[k, d - 1], dev))
         for d, dev in to_y:
             ref = wg.at[k, 1, :, b, y if mine else down(y, d, Y), c]
-            out.append(remote(ref, ref, g1b_s.at[k, d - 1], g1b_r.at[k, d - 1], dev))
+            out.append(remote(ref, ref, g1b_s.at[d - 1], g1b_r.at[k, d - 1], dev))
         return out
 
     def gather_2(k, mine):
         out = []
         for d, dev in to_y:
             ref = wg.at[k, 0, :, :, y if mine else down(y, d, Y), c]
-            out.append(remote(ref, ref, g2a_s.at[k, d - 1], g2a_r.at[k, d - 1], dev))
+            out.append(remote(ref, ref, g2a_s.at[d - 1], g2a_r.at[k, d - 1], dev))
         for d, dev in to_b:
             ref = wg.at[k, 1, :, b if mine else down(b, d, B), :, c]
-            out.append(remote(ref, ref, g2b_s.at[k, d - 1], g2b_r.at[k, d - 1], dev))
+            out.append(remote(ref, ref, g2b_s.at[d - 1], g2b_r.at[k, d - 1], dev))
         return out
 
     def gather_c(k, mine):
         ref = wg.at[k, :, :, :, :, c if mine else oc]
-        return remote(ref, ref, gc_s.at[k], gc_r.at[k], to_c)
-
-    def guarded(fn):
-        def at(k):
-            if isinstance(k, int):
-                if 0 <= k < chunks:
-                    fn(k)
-            else:
-                pl.when(jnp.logical_and(k >= 0, k < chunks))(lambda: fn(k))
-
-        return at
+        return remote(ref, ref, gc_s.at[0], gc_r.at[k], to_c)
+
+    def region(fn):
+        pl.when(dp >= 0)(fn)
 
     def bias_z(d, dev, mine):
         ref = bb.at[a if mine else down(a, d, A), b, y, c]
@@ -164,21 +148,18 @@
         ref = bb.at[:, :, :, c if mine else oc]
         return remote(ref, ref, bc_s.at[0], bc_r.at[0], to_c)
 
-    @guarded
     def ag1(k):
         for d, dev in to_a:
             gather_z(k, d, dev, False).wait_recv()
         for copy in gather_1(k, True):
             copy.start()
 
-    @guarded
     def ag2(k):
         for copy in gather_1(k, False):
             copy.wait_recv()
         for copy in gather_2(k, True):
             copy.start()
 
-    @guarded
     def ag3(k):
         for copy in gather_2(k, False):
             copy.wait_recv()
@@ -201,36 +182,38 @@
             bias_2(d, dev, False).wait_recv()
         bias_c(True).start()
 
-    for copy in weight_loads[:2]:
-        copy.wait()
-    bias_load.wait()
-    for d, dev in to_a:
-        gather_z(0, d, dev, True).start()
-        bias_z(d, dev, True).start()
-    for copy in weight_loads[2:]:
-        copy.wait()
-    for k in range(1, chunks):
+    def agz(k):
+        for copy in weight_loads[2 * k : 2 * k + 2]:
+            copy.wait()
         for d, dev in to_a:
             gather_z(k, d, dev, True).start()
 
+    def bias_agz():
+        spread = lax.rem(lax.broadcasted_iota(jnp.int32, (rows, LANES), 1), rows)
+        spread = (spread == lax.broadcasted_iota(jnp.int32, (rows, LANES), 0)).astype(F32).astype(BF16)
+        own_bias = jnp.broadcast_to(bias[...], (8, rows))
+        bb[a, b, y, c] = jnp.dot(own_bias, spread, preferred_element_type=F32)
+        for d, dev in to_a:
+            bias_z(d, dev, True).start()
+
+    bias_agz()
+    agz(0)
+
     for copy in side_loads:
         copy.wait()
-    for m in range(batches):
-        cot_load(0, m).start()
+    cot_load(0).start()
     bacc[...] = jnp.zeros_like(bacc)
 
     def pooling(m, q):
         s = m * slots + q
         here = pl.multiple_of(q * SLOT, SLOT)
         flat = pl.multiple_of(s * SLOT, SLOT)
-        lists = nbuf[m, pl.ds(here, SLOT), :]
+        listed = nbuf[m, :, pl.ds(here, SLOT)].astype(F32).astype(BF16)
         lane = lax.broadcasted_iota(jnp.int32, (SLOT, SLOT), 1)
         sub = lax.broadcasted_iota(jnp.int32, (SLOT, SLOT), 0)
-        reps = SLOT // lists.shape[1]
-        listed = jnp.concatenate([lists] * reps, axis=1).astype(F32).T.astype(BF16)
         position = sub.astype(F32).astype(BF16)
         counted = jnp.zeros((SLOT, SLOT), BF16)
-        for j in range(lists.shape[1]):
+        for j in range(listed.shape[0]):
             counted = counted + jnp.where(listed[j : j + 1, :] == position, jnp.bfloat16(1), jnp.bfloat16(0))
         counted = counted.astype(F32).T
         ids, alive = sbuf[m : m + 1, pl.ds(here, SLOT)], lbuf[m : m + 1, pl.ds(here, SLOT)]
@@ -248,12 +231,12 @@
         pool_t[:, :, :, pl.ds(flat, SLOT)] = pooled.T.reshape(groups, C, rows, SLOT)
 
     early = {
-        4: [lambda: ag1(0), bias_ag1],
-        7: [lambda: ag1(1)],
-        8: [lambda: ag2(0), bias_ag2],
-        10: [lambda: ag1(2)],
-        11: [lambda: ag2(1)],
-        13: [lambda: ag3(0), bias_ag3, lambda: ag1(3)],
+        1: [bias_ag1, lambda: ag1(0), lambda: agz(1)],
+        6: [bias_ag2, lambda: ag2(0), lambda: agz(2)],
+        8: [lambda: ag1(1)],
+        10: [lambda: agz(3)],
+        12: [lambda: agz(4)],
+        13: [bias_ag3, lambda: ag3(0), lambda: ag1(2), lambda: ag2(1)],
     }
     for m in range(batches):
         feat_loads[m].wait()
@@ -283,10 +266,10 @@
         brow[j] = jnp.broadcast_to(row, (8, LANES))
 
     def reduce_c(k):
-        return remote(csend.at[lax.rem(k, 2)], crecv.at[k], rc_s.at[k], rc_r.at[k], to_c)
+        return remote(csend.at[k % 2], crecv.at[k], rc_s.at[k], rc_r.at[k], to_c)
 
     def reduce_1(k):
-        e = lax.rem(k, 2)
+        e = k % 2
         out_a = [
             remote(s1a.at[e, d - 1], r1a.at[k, d - 1], p1a_s.at[k, d - 1], p1a_r.at[k, d - 1], dev) for d, dev in to_y
         ]
@@ -296,7 +279,7 @@
         return out_a + out_b
 
     def reduce_2(k):
-        e = lax.rem(k, 2)
+        e = k % 2
         out_a = [
             remote(s2a.at[e, d - 1], r2a.at[k, d - 1], p2a_s.at[k, d - 1], p2a_r.at[k, d - 1], dev) for d, dev in to_b
         ]
@@ -306,25 +289,18 @@
         return out_a + out_b
 
     def reduce_z(k):
-        e = lax.rem(k, 2)
+        e = k % 2
         return [remote(sz.at[e, d - 1], rz.at[k, d - 1], pz_s.at[k, d - 1], pz_r.at[k, d - 1], dev) for d, dev in to_a]
 
     def ago(k, n, copies):
-        def wait():
+        if k >= n:
             for copy in copies(k - n):
                 copy.wait_send()
 
-        if isinstance(k, int):
-            if k >= n:
-                wait()
-        else:
-            pl.when(k >= n)(wait)
-
     lo, hi = slice(0, LANES), slice(LANES, CHUNK)
 
-    @guarded
     def rs1(k):
-        t, e = lax.rem(k, RING), lax.rem(k, 2)
+        t, e = k, k % 2
         reduce_c(k).wait_recv()
         ago(k, 2, reduce_1)
         for d, _ in to_y:
@@ -338,9 +314,8 @@
         acc[t, :, :, y, :, lo] = acc[t, :, :, y, :, lo] + crecv[k, :, :, y, :, lo].astype(F32)
         acc[t, :, b, :, :, hi] = acc[t, :, b, :, :, hi] + crecv[k, :, b, :, :, hi].astype(F32)
 
-    @guarded
     def rs2(k):
-        t, e = lax.rem(k, RING), lax.rem(k, 2)
+        t, e = k, k % 2
         for copy in reduce_1(k):
             copy.wait_recv()
         ago(k, 2, reduce_2)
@@ -366,9 +341,8 @@
         acc[t, :, b, y, :, lo] = total_a(b)
         acc[t, :, b, y, :, hi] = total_b(y)
 
-    @guarded
     def rs3(k):
-        t, e = lax.rem(k, RING), lax.rem(k, 2)
+        t, e = k, k % 2
         for copy in reduce_2(k):
             copy.wait_recv()
         ago(k, 2, reduce_z)
@@ -388,12 +362,11 @@
         acc[t, a, b, y] = total(a)
 
     def wout_store(k):
-        cols = pl.ds(pl.multiple_of(k * CHUNK, CHUNK), CHUNK)
-        return pltpu.make_async_copy(wout.at[k], wgrad_out.at[:, cols], wout_sem.at[k])
-
-    @guarded
+        cols = columns(k)
+        return pltpu.make_async_copy(wout.at[k], wgrad_out.at[:, cols], wout_sem.at[0])
+
     def rs4(k):
-        t = lax.rem(k, RING)
+        t = k
         for copy in reduce_z(k):
             copy.wait_recv()
         out = acc[t, a, b, y]
@@ -402,68 +375,73 @@
         wout[k] = out
         wout_store(k).start()
 
-    def columns(k):
-        return pl.ds(pl.multiple_of(k * CHUNK, CHUNK), CHUNK)
-
-    def forward(k, i):
-        e = lax.rem(k, 2)
-        part = pl.ds(i * half, half)
+    def forward(k):
+        e = k % 2
         w = jnp.concatenate([wg[k, h].reshape(D, LANES) for h in range(2)], axis=1)
         offset = jnp.concatenate([brow[2 * k + h][0:1] for h in range(2)], axis=1)
-        preact = jnp.dot(pool[part, :], w, preferred_element_type=F32) + offset
-        squash = jax.nn.sigmoid(preact)
-        active = preact * squash
-        act[e, part, :] = active.astype(BF16)
-        grad = (ct[e, part, :].astype(F32) * (squash + active * (1.0 - squash))).astype(BF16)
-        gp[part, columns(k)] = grad
-        bacc[:, columns(k)] += jnp.sum(grad.astype(F32).reshape(half // 8, 8, CHUNK), axis=0)
+        sums = jnp.zeros((8, CHUNK), F32)
+        for m in range(batches):
+            part = slice(m * local, (m + 1) * local)
+            preact = jnp.dot(pool[part, :], w, preferred_element_type=F32) + offset
+            squash = jax.nn.sigmoid(preact)
+            active = preact * squash
+            act[e, m] = active.astype(BF16)
+            grad = (ct[e, m].astype(F32) * (squash + active * (1.0 - squash))).astype(BF16)
+            gp[part, columns(k)] = grad
+            sums = sums + jnp.sum(grad.astype(F32).reshape(local // 8, 8, CHUNK), axis=0)
+        bacc[:, columns(k)] = sums
 
     def weight_term(k, which):
         left = pool_t[:, which].reshape(plane, N)
         return jnp.dot(left, gp[:, columns(k)], preferred_element_type=F32).reshape(A, B, Y, rows, CHUNK)
 
-    def chunk(k, carry):
-        e, t = lax.rem(k, 2), lax.rem(k, RING)
+    def forward_region(k):
         gather_c(k, False).wait_recv()
-        for m in range(batches):
-            cot_load(k, m).wait()
-
-        @pl.when(k + 1 < chunks)
-        def _():
-            for m in range(batches):
-                cot_load(k + 1, m).start()
-
-        @pl.when(k >= 2)
-        def _():
-            for m in range(batches):
-                act_store(k - 2, m).wait()
-
-        pl.when(k >= 0)(lambda: forward(k, 0))
-        ag2(k + 2)
-        ag3(k + 1)
-        rs1(k - 1)
-        rs4(k - 4)
-        pl.when(k >= 0)(lambda: forward(k, 1))
-        for m in range(batches):
-            act_store(k, m).start()
-        rs2(k - 2)
+        cot_load(k).wait()
+        if k + 1 < chunks:
+            cot_load(k + 1).start()
+        if k >= 2:
+            act_store(k - 2).wait()
+
+    def weight_region(k):
         ago(k, 2, lambda j: [reduce_c(j)])
 
-        @pl.when(k >= 0)
-        def _():
-            csend[e] = weight_term(k, oc).astype(BF16)
-
-        reduce_c(k).start()
-        ag1(k + 4)
-        rs3(k - 3)
-
-        @pl.when(k >= 0)
-        def _():
-            acc[t] = weight_term(k, c)
-
-        return carry
-
-    lax.fori_loop(0, chunks, chunk, 0)
+    def weight_terms(k):
+        csend[k % 2] = weight_term(k, oc).astype(BF16)
+        acc[k] = weight_term(k, c)
+
+    regions = [(0, None), (None, 0), (1, None)] + [(k, k - 1) for k in range(2, chunks)] + [(None, chunks - 1)]
+    plan = [
+        (ag1, {3: 0, 4: 1, 5: 3, 6: 4, 7: 5}),
+        (agz, {5: 0, 6: 1, 7: 2}),
+        (ag3, {1: 1, 2: 2, 3: 3, 4: 4, 5: 5, 6: 6, 7: 7}),
+        (ag2, {2: 0, 3: 2, 4: 3, 5: 4, 6: 5, 7: 6}),
+        (rs4, {}),
+        (rs3, {0: 8, 1: 9}),
+        (rs2, {0: 6, 1: 7, 2: 8, 3: 9}),
+        (rs1, {0: 4, 1: 5, 2: 6, 3: 7, 4: 8, 5: 9}),
+    ]
+    for at, (f, w) in enumerate(regions):
+        for stage, when in plan:
+            for k, ahead in when.items():
+                if ahead == at:
+                    stage(k)
+        if f is not None:
+            forward_region(f)
+        if w is not None:
+            weight_region(w)
+
+        @region
+        def _(f=f, w=w):
+            if f is not None:
+                forward(f)
+            if w is not None:
+                weight_terms(w)
+
+        if f is not None:
+            act_store(f).start()
+        if w is not None:
+            reduce_c(w).start()
 
     def bred_c():
         return remote(bt.at[:, :, :, oc], brc, dc_s.at[0], dc_r.at[0], to_c)
@@ -542,12 +520,16 @@
             out = jnp.dot(jnp.concatenate([left, left], axis=1), right, preferred_element_type=F32)
             fout[e, part, :] = out.astype(BF16)
 
-    late = {
-        0: [lambda: rs1(chunks - 1), bias_rs1, lambda: rs2(chunks - 2), lambda: rs3(chunks - 3), lambda: rs4(chunks - 4)],
-        2: [lambda: rs2(chunks - 1), bias_rs2, lambda: rs3(chunks - 2), lambda: rs4(chunks - 3)],
-        5: [lambda: rs3(chunks - 1), bias_rs3, lambda: rs4(chunks - 2)],
-        8: [lambda: rs4(chunks - 1), bias_rs4],
-    }
+    late = [
+        (rs1, {6: 0, 7: 2}),
+        (rs2, {4: 0, 5: 1, 6: 4, 7: 6}),
+        (rs3, {2: 0, 3: 1, 4: 3, 5: 5, 6: 7, 7: 9}),
+        (rs4, {0: 0, 1: 1, 2: 3, 3: 4, 4: 6, 5: 8, 6: 10, 7: 11}),
+        (lambda _: bias_rs1(), {0: 1}),
+        (lambda _: bias_rs2(), {0: 4}),
+        (lambda _: bias_rs3(), {0: 7}),
+        (lambda _: bias_rs4(), {0: 10}),
+    ]
     steps = A * batches
 
     def last(i, carry):
@@ -557,13 +539,9 @@
 
         pl.when(i >= 0)(lambda: feature_grad(i))
         fout_store(i).start()
-        for at, events in late.items():
-
-            @pl.when(i == at)
-            def _(events=events):
-                for event in events:
-                    event()
-
+        for stage, when in late:
+            for k, at in when.items():
+                pl.when(i == at)(functools.partial(stage, k))
         return carry
 
     lax.fori_loop(0, steps, last, 0)
@@ -571,20 +549,23 @@
     for i in (steps - 2, steps - 1):
         fout_store(i).wait()
     for k in (chunks - 2, chunks - 1):
-        for m in range(batches):
-            act_store(k, m).wait()
+        act_store(k).wait()
         for copy in [reduce_c(k)] + reduce_1(k) + reduce_2(k) + reduce_z(k):
             copy.wait_send()
 
-    def drained(k, carry):
-        wout_store(k).wait()
-        for d, dev in to_a:
-            gather_z(k, d, dev, True).wait_send()
-        for copy in gather_1(k, True) + gather_2(k, True) + [gather_c(k, True)]:
-            copy.wait_send()
-        return carry
-
-    lax.fori_loop(0, chunks, drained, 0)
+    def drained(ref, sem, dev):
+        remote(ref, ref, sem, sem, dev).wait_send()
+
+    pltpu.make_async_copy(wgrad_out, wgrad_out, wout_sem.at[0]).wait()
+    for d, dev in to_a:
+        drained(wg.at[:, :, a, b, y, c], gz_s.at[d - 1], dev)
+    for d, dev in to_b:
+        drained(wg.at[:, 0, :, b, y, c], g1a_s.at[d - 1], dev)
+        drained(wg.at[:, 1, :, b, :, c], g2b_s.at[d - 1], dev)
+    for d, dev in to_y:
+        drained(wg.at[:, 1, :, b, y, c], g1b_s.at[d - 1], dev)
+        drained(wg.at[:, 0, :, :, y, c], g2a_s.at[d - 1], dev)
+    drained(wg.at[:, :, :, :, :, c], gc_s.at[0], to_c)
     for d, dev in to_a:
         bias_z(d, dev, True).wait_send()
     for d, dev in to_b:
@@ -604,7 +585,7 @@
     chunks = D // CHUNK
     groups = A * B * Y
     wide = D // A
-    tile = jnp.broadcast_to(jnp.tile(bias.astype(F32), LANES // rows)[None], (8, LANES))
+    neighbours = jnp.swapaxes(neighbours, 1, 2)
     any_spec = pl.BlockSpec(memory_space=pl.ANY)
     vmem, dma = pltpu.VMEM, pltpu.SemaphoreType.DMA
     scratch = [
@@ -612,9 +593,9 @@
         vmem((N, D), BF16),
         vmem((groups, C, rows, N), BF16),
         vmem((N, D), BF16),
-        vmem((2, N, CHUNK), BF16),
-        vmem((2, N, CHUNK), BF16),
-        vmem((RING, A, B, Y, rows, CHUNK), F32),
+        vmem((2, batches, local, CHUNK), BF16),
+        vmem((2, batches, local, CHUNK), BF16),
+        vmem((chunks, A, B, Y, rows, CHUNK), F32),
         vmem((2, A, B, Y, rows, CHUNK), BF16),
         vmem((chunks, A, B, Y, rows, CHUNK), BF16),
         vmem((2, Y - 1, A, B, rows, LANES), BF16),
@@ -644,18 +625,34 @@
         vmem((B - 1, A, 8, LANES), F32),
         vmem((A - 1, 8, LANES), F32),
         dma((2, 2 * chunks)),
-        dma((2, batches)),
-        dma((2, batches)),
         dma((2,)),
-        dma((chunks,)),
+        dma((2,)),
+        dma((2,)),
+        dma((1,)),
     ]
-    for shape in (
-        [(chunks, A - 1), (chunks, B - 1), (chunks, Y - 1), (chunks, Y - 1), (chunks, B - 1), (chunks,)]
-        + [(chunks,), (chunks, Y - 1), (chunks, B - 1), (chunks, B - 1), (chunks, Y - 1), (chunks, A - 1)]
-        + [(A - 1,), (B - 1,), (Y - 1,), (1,)]
-        + [(1,), (Y - 1,), (B - 1,), (A - 1,)]
+    for sent, received in (
+        ((A - 1,), (chunks, A - 1)),
+        ((B - 1,), (chunks, B - 1)),
+        ((Y - 1,), (chunks, Y - 1)),
+        ((Y - 1,), (chunks, Y - 1)),
+        ((B - 1,), (chunks, B - 1)),
+        ((1,), (chunks,)),
+        ((chunks,), (chunks,)),
+        ((chunks, Y - 1), (chunks, Y - 1)),
+        ((chunks, B - 1), (chunks, B - 1)),
+        ((chunks, B - 1), (chunks, B - 1)),
+        ((chunks, Y - 1), (chunks, Y - 1)),
+        ((chunks, A - 1), (chunks, A - 1)),
+        ((A - 1,), (A - 1,)),
+        ((B - 1,), (B - 1,)),
+        ((Y - 1,), (Y - 1,)),
+        ((1,), (1,)),
+        ((1,), (1,)),
+        ((Y - 1,), (Y - 1,)),
+        ((B - 1,), (B - 1,)),
+        ((A - 1,), (A - 1,)),
     ):
-        scratch += [dma(shape), dma(shape)]
+        scratch += [dma(sent), dma(received)]
     act, fgrad, wgrad, bgrad = pl.pallas_call(
         functools.partial(kernel, dims),
         out_shape=[
@@ -664,7 +661,7 @@
             jax.ShapeDtypeStruct(weight.shape, F32),
             jax.ShapeDtypeStruct((1, rows), F32),
         ],
-        in_specs=[any_spec] * 7,
+        in_specs=[any_spec] * 6 + [pl.BlockSpec(memory_space=pltpu.VMEM)],
         out_specs=[any_spec] * 3 + [pl.BlockSpec(memory_space=pltpu.VMEM)],
         scratch_shapes=scratch,
         compiler_params=pltpu.CompilerParams(
@@ -673,7 +670,7 @@
         cost_estimate=pl.CostEstimate(
             flops=6 * N * D * D, bytes_accessed=8 * N * D, transcendentals=N * D
         ),
-    )(features, cotangent, neighbours, segments, live, weight, tile)
+    )(features, cotangent, neighbours, segments, live, weight, bias.reshape(1, rows))
     return act, fgrad, wgrad, bgrad.reshape(rows)
 
 

time: 127 us -> 112 us (0.88)
  Pallas kernels: 110 us -> 98.8 us
  local copies, waits for them, and re-layouts: 16.2 us -> 12.7 us
    pallas_call x1, Pallas kernels: 110 us -> 98.8 us  [per_device(): pl.pallas_call(functools.partial(kernel, dims), out_shape=[jax.ShapeDtype...]
    unnamed x11 -> x10, local copies, waits for them, and re-layouts: 14.9 us -> 12.7 us
where the time goes in v1:
time: 112 us
  Pallas kernels  98.8 us (88%)
  local copies, waits for them, and re-layouts  12.7 us (11%)
    pallas_call x1, Pallas kernels, per_device(): pl.pallas_call(functools.partial(kernel, dims), out_shape=[jax.ShapeDtype...  98.8 us
    unnamed x10, local copies, waits for them, and re-layouts  12.7 us

profile of v1, /device:TPU:0, one launch (start us, length us, event | category | flops | bytes accessed | tf_op | source)
XLA Modules:
  0.0 112.2 jit_solution(3048749801872963139)
XLA Ops:
  0.6 98.8 %shard_map.102 = (bf16[3,640,2048]{2,1,0:T(8,128)(2,1)}, bf16[3,640,2048]{2,1,0:T(8,128)(2,1)}, f32[64,2048]{1,0:T(8,128)}, f32[1,64]{1,0:T(1,128)}) custom-call(bf16[3,640,2048]{2,1,0:T(8,128)(2,1)} %feat.1, bf16[3,640,2048]{2,1,0:T(8,128)(2,1)} %cot.1, s32[3,32,640]{2,1,0:T(8,128)} %bitcast.3, s32[3,640]{1,0:T(4,128)} %seg.1, s32[3,640]{1,0:T(4,128)} %live.1, ...), custom_call_target="tpu_custom_call" | custom-call | flops 48318382080 | bytes 31457280 | tf_op jit(solution)/shard_map/pallas_call | solution.py:656
  99.5 0.0 copy-start
  99.5 8.1 %copy.15 = bf16[3,640,2048]{2,1,0:T(8,128)(2,1)} copy(bf16[3,640,2048]{2,1,0:T(8,128)(2,1)} %get-tuple-element.16) | data formatting | bytes 15728640
  107.6 0.0 copy-done
  107.6 0.0 copy-start.1
  107.6 0.0 copy-start.2
  107.6 3.2 %copy.16 = bf16[3,640,2048]{2,1,0:T(8,128)(2,1)} copy(bf16[3,640,2048]{2,1,0:T(8,128)(2,1)S(1)} %copy-done) | data formatting | bytes 15728640
  110.9 0.0 copy-done.1
  110.9 0.8 copy.17
  111.7 0.0 copy-done.2
  111.7 0.5 copy.18
Async XLA Ops:
  99.5 8.1 %copy-start = (bf16[3,640,2048]{2,1,0:T(8,128)(2,1)S(1)}, bf16[3,640,2048]{2,1,0:T(8,128)(2,1)}, u32[]{:S(2)}) copy-start(bf16[3,640,2048]{2,1,0:T(8,128)(2,1)} %get-tuple-element.17) | copy-start | bytes 23592964
  107.6 3.2 %copy-start.1 = (f32[64,2048]{1,0:T(8,128)S(1)}, f32[64,2048]{1,0:T(8,128)}, u32[]{:S(2)}) copy-start(f32[64,2048]{1,0:T(8,128)} %get-tuple-element.18) | copy-start | bytes 1572868
  107.6 4.0 %copy-start.2 = (f32[1,64]{1,0:T(1,128)S(1)}, f32[1,64]{1,0:T(1,128)}, u32[]{:S(2)}) copy-start(f32[1,64]{1,0:T(1,128)} %get-tuple-element.11) | copy-start | bytes 772
